TPU v7x, 32 devices: a whole 2x2x4 slice. The times are simulated.
32 devices in a mesh: groups: 2 (over y), chan: 4 (over z), tm: 2 (over x), band: 2 (over core).
Axes of the slice: x: 2, y: 2, z: 4, core: 2. Of those that a mesh axis runs over, the one named last changes fastest.
Arguments:
- recording: float32 [1024, 2048], P(('groups', 'chan'), 'tm'), parts along dimension 0, may hold values from -460 to 460
- tau_index: int32 [1024], P(('groups', 'chan')), parts along dimension 0, may hold values from 0 to 7
- pair_offset: int32 [4, 4], replicated, may hold values from -1 to 3, as said below
Outputs:
- correlations: float32 [8, 4, 3, 128, 128], P(('groups', 'chan'), None, None, ('tm', 'band')), parts along dimension 0
There are 2 independent parts, one for each index of `groups`. A program takes and returns all parts, laid end to end along the dimension named above; an argument that names none is the same for every part. Nothing has to cross between parts.
Inputs may be any that keep to these rules, and one draw needn't show every extreme that they name: pair_offset[i, q] is an offset of 1 to 3 blocks for q below the row's partner count, and -1 from there on; every row has 1 to 4 partners.
All inputs are finite; a program needn't handle non-finite values.
Results may differ from a plain program's by a relative error of at most 0.006.
Values may be sent and summed in bfloat16 or wider, within the bound.
A program may use at most 64 MiB of HBM per device.

v0:
```python
import math
import jax
import jax.numpy as jnp
from jax import lax
from jax.sharding import PartitionSpec as P

BLK = 128
HALO_CH = 64
HALO_T = 256
LAGS = 3
QMAX = 4


def from_behind(block, axis, distance):
    devices = range(lax.axis_size(axis))
    route = [(i - distance, i) for i in devices if i - distance in devices]
    return lax.ppermute(block, axis, route)


def padded_2(block, sides, width):
    for axis, dim in sides:
        count = lax.axis_size(axis)
        forward = [(i, i + 1) for i in range(count - 1)]
        backward = [(target, source) for source, target in forward]
        low = lax.ppermute(
            lax.slice_in_dim(block, block.shape[dim] - width, None, axis=dim), axis, forward
        )
        high = lax.ppermute(lax.slice_in_dim(block, 0, width, axis=dim), axis, backward)
        block = jnp.concatenate([low, block, high], axis=dim)
    return block


def slide_total(padded, reach, size, axis):
    zero_shape = list(padded.shape)
    zero_shape[axis] = 1
    running = jnp.concatenate(
        [jnp.zeros(zero_shape, jnp.float32), jnp.cumsum(padded, axis=axis)], axis=axis
    )
    upper = lax.slice_in_dim(running, 2 * reach + 1, 2 * reach + 1 + size, axis=axis)
    lower = lax.slice_in_dim(running, 0, size, axis=axis)
    return upper - lower


def spatial_filter(padded, center, counted):
    total = slide_total(padded, HALO_CH, center.shape[0], 0)
    return center - total / counted[:, None]


def amplitude_norm(padded, center):
    total = slide_total(jnp.abs(padded), HALO_T, center.shape[1], 1)
    return center / (total / (2.0 * HALO_T + 1.0) + 1e-06)


def shards(recording, tau_index, pair_offset):
    channels, samples = recording.shape
    chan_count = lax.axis_size("chan")
    time_count = lax.axis_size("tm")
    band_count = lax.axis_size("band")
    chan_pos = lax.axis_index("chan")
    time_pos = lax.axis_index("tm")
    band_pos = lax.axis_index("band")
    all_channels = channels * chan_count
    all_samples = samples * time_count
    kept_bins = all_samples // 4
    first_bin = kept_bins // 4
    band_bins = kept_bins // band_count
    device_bins = band_bins // time_count
    decay = jnp.exp(-1.0 / (2.0 * 2.0 ** (tau_index.astype(jnp.float32) / 2.0)))[:, None]
    rows_global = chan_pos * channels + jnp.arange(channels)
    counted = (
        jnp.minimum(rows_global, HALO_CH) + jnp.minimum(all_channels - 1 - rows_global, HALO_CH) + 1
    ).astype(jnp.float32)
    previous = from_behind(recording[:, samples - 1 :], "tm", 1)
    deconv = recording - decay * jnp.concatenate([previous, recording[:, : samples - 1]], axis=1)
    deconv_wide = padded_2(deconv, (("chan", 0),), HALO_CH)
    filtered = spatial_filter(deconv_wide, deconv, counted)
    filtered_wide = padded_2(filtered, (("tm", 1),), HALO_T)
    normed = amplitude_norm(filtered_wide, filtered)
    time_global = time_pos * samples + jnp.arange(samples)
    sub_rows = math.gcd(device_bins * lax.axis_size("tm"), 128)
    pieces = device_bins * lax.axis_size("tm") // sub_rows

    def one_piece(piece_idx):
        bins_here = first_bin + band_pos * band_bins + piece_idx * sub_rows + jnp.arange(sub_rows)
        turns = bins_here[:, None] * time_global[None, :] % all_samples
        angle = 2.0 * jnp.pi / all_samples * turns.astype(jnp.float32)
        dims = (((1,), (1,)), ((), ()))
        real_part = lax.dot_general(
            jnp.cos(angle),
            normed,
            dims,
            precision=lax.Precision.HIGHEST,
            preferred_element_type=jnp.float32,
        )
        imag_part = -lax.dot_general(
            jnp.sin(angle),
            normed,
            dims,
            precision=lax.Precision.HIGHEST,
            preferred_element_type=jnp.float32,
        )
        return jnp.stack([real_part, imag_part], axis=1)

    stacked = lax.map(one_piece, jnp.arange(pieces))
    spectra = lax.psum_scatter(
        stacked.reshape(device_bins * lax.axis_size("tm"), 2, channels),
        "tm",
        scatter_dimension=0,
        tiled=True,
    )
    local_power = jnp.sum(spectra * spectra, axis=(0, 1))
    power = lax.psum(local_power, ("tm", "band"))
    factor = lax.rsqrt(power / kept_bins + 1e-06)
    white = (spectra * factor[None, None, :]).astype(jnp.bfloat16)
    bins_mine = first_bin + band_pos * band_bins + time_pos * device_bins + jnp.arange(device_bins)
    lagged = jnp.arange(LAGS) - LAGS // 2
    phase = (
        2.0
        * jnp.pi
        / all_samples
        * (bins_mine[:, None] * lagged[None, :] % all_samples).astype(jnp.float32)
    )
    cosine = jnp.cos(phase)[:, :, None]
    sine = jnp.sin(phase)[:, :, None]
    white_f = white.astype(jnp.float32)
    real_shift = white_f[:, 0, None, :] * cosine - white_f[:, 1, None, :] * sine
    imag_shift = white_f[:, 0, None, :] * sine + white_f[:, 1, None, :] * cosine
    shifted = jnp.stack([real_shift, imag_shift], axis=1).astype(jnp.bfloat16)
    own_blocks = channels // BLK
    all_blocks = all_channels // BLK
    my_offsets = lax.dynamic_slice_in_dim(pair_offset, chan_pos * own_blocks, own_blocks, 0)
    left_blocks = [shifted.reshape(2 * device_bins, LAGS * BLK)]
    cc_scale = 1.0 / math.sqrt(kept_bins)
    initial = tuple(
        (jnp.zeros((LAGS * BLK, BLK), jnp.float32) for slot_all in range(own_blocks * QMAX))
    )
    piece = lax.all_gather(white, "chan", axis=2, tiled=True)
    width = piece.shape[2]
    updated = []
    for slot_idx in range(QMAX):
        offset = my_offsets[0, slot_idx]
        partner = (chan_pos * own_blocks + 0 + jnp.maximum(offset, 0)) % all_blocks
        local_col = partner * BLK
        present = (offset >= 0) & (local_col >= 0) & (local_col < width)
        clipped = jnp.clip(local_col, 0, width - BLK)
        right = lax.dynamic_slice_in_dim(piece, clipped, BLK, 2)
        right = right.reshape(2 * device_bins, BLK)

        def compute(previous_value, left=left_blocks[0], right=right):
            product = lax.dot_general(
                left, right, (((0,), (0,)), ((), ())), preferred_element_type=jnp.float32
            )
            return product * cc_scale

        def keep(previous_value):
            return previous_value

        updated.append(lax.cond(present, compute, keep, initial[slot_idx]))
    gathered = tuple(updated)
    stacked_cc = jnp.stack(gathered).reshape(own_blocks, QMAX, LAGS, BLK, BLK)
    return lax.psum_scatter(stacked_cc, ("tm", "band"), scatter_dimension=3, tiled=True)


def solution(mesh):
    return jax.shard_map(
        shards,
        mesh=mesh,
        in_specs=(P(("groups", "chan"), "tm"), P(("groups", "chan")), P()),
        out_specs=P(("groups", "chan"), None, None, ("tm", "band"), None),
        check_vma=False,
    )
```

profile of v0, /device:TPU:0, one launch (start us, length us, event | category | flops | bytes accessed | tf_op | source)
XLA Modules:
  0.0 122.5 jit_solution(3115787574492478725)
XLA Ops:
  6.5 0.9 slice.63
  7.5 4.8 %collective-permute-start = (f32[128,1]{1,0:T(8,128)S(1)}, f32[128,1]{1,0:T(8,128)S(1)}, u32[]{:S(2)}, u32[]{:S(2)}) collective-permute-start(f32[128,1]{1,0:T(8,128)S(1)} %slice.63), channel_id=1, source_target_pairs={{0,2},{1,3},{4,6},{5,7},{8,10},{9,11},{12,14},{13,15},{16,18},{17,... | collective-permute-start | bytes 1544 | tf_op jit(solution)/shard_map/ppermute | solution.py:17
  12.3 0.7 divide_exponential_fusion
  13.0 1.2 collective-permute-done
  14.2 1.4 %fusion.34 = f32[128,1024]{1,0:T(8,128)S(1)} fusion(f32[128,1024]{1,0:T(8,128)} %param.13, f32[128,1023]{1,0:T(8,128)} %bitcast.94, f32[128,1]{1,0:T(8,128)S(1)} %collective-permute-done, f32[128]{0:T(128)S(1)} %divide_exponential_fusion), kind=kLoop, calls=%fused_computation.55 | loop fusion | flops 393216 | bytes 1573376 | tf_op jit(solution)/shard_map/sub | solution.py:74
  15.7 3.5 %collective-permute-start.1 = (f32[64,1024]{1,0:T(8,128)S(1)}, f32[64,1024]{1,0:T(8,128)S(1)}, u32[]{:S(2)}, u32[]{:S(2)}) collective-permute-start(f32[64,1024]{1,0:T(8,128)S(1)} %get-tuple-element.262), channel_id=1, source_target_pairs={{0,4},{4,8},{8,12},{1,5},{5,9},{9,13},{2,6},{6,10},{10,14},{3,7},{... | collective-permute-start | bytes 786440 | tf_op jit(solution)/shard_map/ppermute | solution.py:25
  19.2 1.3 %collective-permute-start.2 = (f32[64,1024]{1,0:T(8,128)S(1)}, f32[64,1024]{1,0:T(8,128)S(1)}, u32[]{:S(2)}, u32[]{:S(2)}) collective-permute-start(f32[64,1024]{1,0:T(8,128)S(1)} %get-tuple-element.263), channel_id=1, source_target_pairs={{4,0},{8,4},{12,8},{5,1},{9,5},{13,9},{6,2},{10,6},{14,10},{7,3},{... | collective-permute-start | bytes 786440 | tf_op jit(solution)/shard_map/ppermute | solution.py:28
  20.5 3.4 %collective-permute-done.1 = f32[64,1024]{1,0:T(8,128)S(1)} collective-permute-done((f32[64,1024]{1,0:T(8,128)S(1)}, f32[64,1024]{1,0:T(8,128)S(1)}, u32[]{:S(2)}, u32[]{:S(2)}) %collective-permute-start.1) | collective-permute-done | bytes 262176 | tf_op jit(solution)/shard_map/ppermute | solution.py:25
  23.9 4.1 %collective-permute-done.2 = f32[64,1024]{1,0:T(8,128)S(1)} collective-permute-done((f32[64,1024]{1,0:T(8,128)S(1)}, f32[64,1024]{1,0:T(8,128)S(1)}, u32[]{:S(2)}, u32[]{:S(2)}) %collective-permute-start.2) | collective-permute-done | bytes 262176 | tf_op jit(solution)/shard_map/ppermute | solution.py:28
  28.1 0.8 fusion.25
  29.6 4.0 %collective-permute-start.3 = (f32[128,256]{1,0:T(8,128)S(1)}, f32[128,256]{1,0:T(8,128)S(1)}, u32[]{:S(2)}, u32[]{:S(2)}) collective-permute-start(f32[128,256]{1,0:T(8,128)S(1)} %get-tuple-element.260), channel_id=1, source_target_pairs={{0,2},{1,3},{4,6},{5,7},{8,10},{9,11},{12,14},{13,15},{16,18},{17,... | collective-permute-start | bytes 393224 | tf_op jit(solution)/shard_map/ppermute | solution.py:25
  33.6 1.3 %collective-permute-start.4 = (f32[128,256]{1,0:T(8,128)S(1)}, f32[128,256]{1,0:T(8,128)S(1)}, u32[]{:S(2)}, u32[]{:S(2)}) collective-permute-start(f32[128,256]{1,0:T(8,128)S(1)} %get-tuple-element.261), channel_id=1, source_target_pairs={{2,0},{3,1},{6,4},{7,5},{10,8},{11,9},{14,12},{15,13},{18,16},{19,... | collective-permute-start | bytes 393224 | tf_op jit(solution)/shard_map/ppermute | solution.py:28
  34.9 1.2 collective-permute-done.3
  36.0 4.4 %collective-permute-done.4 = f32[128,256]{1,0:T(8,128)S(1)} collective-permute-done((f32[128,256]{1,0:T(8,128)S(1)}, f32[128,256]{1,0:T(8,128)S(1)}, u32[]{:S(2)}, u32[]{:S(2)}) %collective-permute-start.4) | collective-permute-done | bytes 131104 | tf_op jit(solution)/shard_map/ppermute | solution.py:28
  42.1 13.2 %while.13 = (s32[]{:T(128)}, f32[2,128,2,128]{3,1,0,2:T(8,128)S(1)}, s32[2]{0:T(128)S(1)}, s32[]{:T(128)}, f32[128,1024]{1,0:T(8,128)S(1)}, /*index=5*/s32[]{:T(128)}, s32[]{:T(128)}, s32[1]{0:T(128)}) while((s32[]{:T(128)}, f32[2,128,2,128]{3,1,0,2:T(8,128)S(1)}, s32[2]{0:T(128)S(1)}, s32[]{:T(128)}, f32[128,1024]{1,0:T(8,128)S(1)}, ...), condition=%wide.region_5.6_spmd.clone, body=%wide.region_4.5_spmd.clone.sunk | while | flops 406373504 | bytes 1455749 | solution.py:104
  43.5 2.6 %convolution_bitcast_fusion.2 = f32[128,1,128]{2,0,1:T(8,128)S(1)} fusion(f32[128,1024]{1,0:T(8,128)S(1)} %get-tuple-element.331, s32[1024]{0:T(1024)S(1)} %iota_add_fusion.6, s32[128]{0:T(128)S(1)} %iota_add_fusion.7), kind=kOutput, calls=%fused_computation.15.clone.1 | convolution fusion | flops 203161600 | bytes 594432 | tf_op jit(solution)/shard_map/while/body/eval_jaxpr/dot_general | solution.py:88
  46.1 2.6 %fusion.64 = f32[128,1,128]{2,0,1:T(8,128)S(1)} fusion(f32[128,1024]{1,0:T(8,128)S(1)} %get-tuple-element.331, s32[1024]{0:T(1024)S(1)} %iota_add_fusion.6, s32[128]{0:T(128)S(1)} %iota_add_fusion.7), kind=kOutput, calls=%fused_computation.14.clone.1 | convolution fusion | flops 203177984 | bytes 594432 | tf_op jit(solution)/shard_map/while/body/eval_jaxpr/dot_general | solution.py:95
  50.1 2.6 %convolution_bitcast_fusion.2 = f32[128,1,128]{2,0,1:T(8,128)S(1)} fusion(f32[128,1024]{1,0:T(8,128)S(1)} %get-tuple-element.331, s32[1024]{0:T(1024)S(1)} %iota_add_fusion.6, s32[128]{0:T(128)S(1)} %iota_add_fusion.7), kind=kOutput, calls=%fused_computation.15.clone.1 | convolution fusion | flops 203161600 | bytes 594432 | tf_op jit(solution)/shard_map/while/body/eval_jaxpr/dot_general | solution.py:88
  52.7 2.6 %fusion.64 = f32[128,1,128]{2,0,1:T(8,128)S(1)} fusion(f32[128,1024]{1,0:T(8,128)S(1)} %get-tuple-element.331, s32[1024]{0:T(1024)S(1)} %iota_add_fusion.6, s32[128]{0:T(128)S(1)} %iota_add_fusion.7), kind=kOutput, calls=%fused_computation.14.clone.1 | convolution fusion | flops 203177984 | bytes 594432 | tf_op jit(solution)/shard_map/while/body/eval_jaxpr/dot_general | solution.py:95
  55.3 0.7 copy-done.1
  56.1 0.7 fusion.43
  62.3 4.9 %reduce-scatter.3.cloned.1.call-done = f32[128,2,128]{2,0,1:T(8,128)} async-done(((f32[256,2,128]{2,0,1:T(8,128)}), f32[128,2,128]{2,0,1:T(8,128)}) %reduce-scatter.3.cloned.1.call-update) | async-done | bytes 131088 | tf_op jit(solution)/shard_map/reduce_scatter | solution.py:105
  67.1 1.0 multiply_reduce_fusion
  68.1 5.8 %psum.7 = f32[128]{0:T(128)S(1)} all-reduce(f32[128]{0:T(128)S(1)} %multiply_reduce_fusion), channel_id=1, replica_groups=mesh['groups'=2,'chan'=4,'tm'=2,'band'=2] {'tm','band'}, use_global_device_ids=true, to_apply=%region_8.9 | all-reduce | flops 128 | bytes 1024 | tf_op jit(solution)/shard_map/psum | solution.py:112
  73.9 0.9 fusion.40
  75.4 13.0 %all_gather.3 = bf16[128,2,512]{2,0,1:T(8,128)(2,1)S(1)} all-gather(bf16[128,2,128]{2,0,1:T(8,128)(2,1)S(1)} %get-tuple-element.259), channel_id=1, replica_groups=mesh['groups'=2,'chan'=4,'tm'=2,'band'=2] {'chan'}, dimensions={2}, use_global_device_ids=true | all-gather | bytes 327680 | tf_op jit(solution)/shard_map/all_gather | solution.py:137
  88.4 0.8 conditional.4
  89.2 0.8 conditional.5
  90.0 0.8 conditional.6
  90.8 0.8 conditional.7
  91.6 1.0 pad_maximum_fusion.1
  92.6 23.1 %reduce-scatter.5.cloned.1.call-done = f32[1,4,3,32,128]{4,3,2,1,0:T(8,128)} async-done(((f32[1,4,3,128,128]{4,3,2,1,0:T(8,128)}), f32[1,4,3,32,128]{4,3,2,1,0:T(8,128)}) %reduce-scatter.5.cloned.1.call-update) | async-done | bytes 196624 | tf_op jit(solution)/shard_map/reduce_scatter | solution.py:161
  (64 shorter events, 7.8 us)
Async XLA Ops:
  6.5 28.3 %copy-start = (s32[4,4]{1,0:T(4,128)S(1)}, s32[4,4]{1,0:T(4,128)}, u32[]{:S(2)}) copy-start(s32[4,4]{1,0:T(4,128)} %param.15) | copy-start | bytes 196
  6.5 60.6 %reduce-scatter.3.cloned.1.call-start = ((), (), s32[]{:S(2)}) async-start(), calls=%async_computation.2 | async-start | bytes 393216 | tf_op jit(solution)/shard_map/reduce_scatter | solution.py:105
  7.5 6.7 %collective-permute-start = (f32[128,1]{1,0:T(8,128)S(1)}, f32[128,1]{1,0:T(8,128)S(1)}, u32[]{:S(2)}, u32[]{:S(2)}) collective-permute-start(f32[128,1]{1,0:T(8,128)S(1)} %slice.63), channel_id=1, source_target_pairs={{0,2},{1,3},{4,6},{5,7},{8,10},{9,11},{12,14},{13,15},{16,18},{17,... | collective-permute-start | bytes 1544 | tf_op jit(solution)/shard_map/ppermute | solution.py:17
  15.7 8.2 %collective-permute-start.1 = (f32[64,1024]{1,0:T(8,128)S(1)}, f32[64,1024]{1,0:T(8,128)S(1)}, u32[]{:S(2)}, u32[]{:S(2)}) collective-permute-start(f32[64,1024]{1,0:T(8,128)S(1)} %get-tuple-element.262), channel_id=1, source_target_pairs={{0,4},{4,8},{8,12},{1,5},{5,9},{9,13},{2,6},{6,10},{10,14},{3,7},{... | collective-permute-start | bytes 786440 | tf_op jit(solution)/shard_map/ppermute | solution.py:25
  19.2 8.8 %collective-permute-start.2 = (f32[64,1024]{1,0:T(8,128)S(1)}, f32[64,1024]{1,0:T(8,128)S(1)}, u32[]{:S(2)}, u32[]{:S(2)}) collective-permute-start(f32[64,1024]{1,0:T(8,128)S(1)} %get-tuple-element.263), channel_id=1, source_target_pairs={{4,0},{8,4},{12,8},{5,1},{9,5},{13,9},{6,2},{10,6},{14,10},{7,3},{... | collective-permute-start | bytes 786440 | tf_op jit(solution)/shard_map/ppermute | solution.py:28
  29.6 6.5 %collective-permute-start.3 = (f32[128,256]{1,0:T(8,128)S(1)}, f32[128,256]{1,0:T(8,128)S(1)}, u32[]{:S(2)}, u32[]{:S(2)}) collective-permute-start(f32[128,256]{1,0:T(8,128)S(1)} %get-tuple-element.260), channel_id=1, source_target_pairs={{0,2},{1,3},{4,6},{5,7},{8,10},{9,11},{12,14},{13,15},{16,18},{17,... | collective-permute-start | bytes 393224 | tf_op jit(solution)/shard_map/ppermute | solution.py:25
  33.6 6.9 %collective-permute-start.4 = (f32[128,256]{1,0:T(8,128)S(1)}, f32[128,256]{1,0:T(8,128)S(1)}, u32[]{:S(2)}, u32[]{:S(2)}) collective-permute-start(f32[128,256]{1,0:T(8,128)S(1)} %get-tuple-element.261), channel_id=1, source_target_pairs={{2,0},{3,1},{6,4},{7,5},{10,8},{11,9},{14,12},{15,13},{18,16},{19,... | collective-permute-start | bytes 393224 | tf_op jit(solution)/shard_map/ppermute | solution.py:28
  55.3 0.7 copy-start.1
  56.0 59.6 %reduce-scatter.5.cloned.1.call-start = ((), (), s32[]{:S(2)}) async-start(), calls=%async_computation.3 | async-start | bytes 983040 | tf_op jit(solution)/shard_map/reduce_scatter | solution.py:161
Sparse Core Ops, SparseCore 0:
  56.1 10.9 reduce-scatter.2
  92.7 22.9 reduce-scatter.4
where the time goes:
time: 123 us
  waiting for transfers between devices  42.2 us (34%)
  between operations  18.9 us (15%)
  blocking collectives  18.8 us (15%)
  starting transfers between devices  14.9 us (12%)
  matrix products  11.1 us (9%)
  other arithmetic  7.65 us (6%)
  local copies, waits for them, and re-layouts  7.28 us (6%)
  loops' own time  1.66 us (1%)
    reduce_scatter x1, waiting for transfers between devices, shards(): lax.psum_scatter(stacked_cc, ('tm', 'band'), scatter_dimension=3, tiled=T...  23.1 us
    all_gather x1, blocking collectives, shards(): piece = lax.all_gather(white, 'chan', axis=2, tiled=True)  13 us
    ppermute x2, waiting for transfers between devices, padded_2(): lax.ppermute(lax.slice_in_dim(block, 0, width, axis=dim), axis, backward)  8.49 us
    ppermute x2, starting transfers between devices, padded_2(): lax.ppermute(lax.slice_in_dim(block, block.shape[dim] - width, None, axis...  7.47 us
    psum x1, blocking collectives, shards(): power = lax.psum(local_power, ('tm', 'band'))  5.75 us
    dot_general x2, matrix products, one_piece(): lax.dot_general(jnp.sin(angle), normed, dims, precision=lax.Precision.HIG...  5.16 us
    dot_general x2, matrix products, one_piece(): lax.dot_general(jnp.cos(angle), normed, dims, precision=lax.Precision.HIG...  5.13 us
    reduce_scatter x1, waiting for transfers between devices, shards(): lax.psum_scatter(stacked.reshape(device_bins * lax.axis_size('tm'), 2, ch...  4.85 us
  transfers between devices with their start and end apart: 7, of which 7 were waited for; matrix products, arithmetic and copies ran while one was open for 1% of the time, Pallas kernels for 0%

commit v1 on v0

--- a/solution.py
+++ b/solution.py
@@ -134,7 +134,24 @@
     initial = tuple(
         (jnp.zeros((LAGS * BLK, BLK), jnp.float32) for slot_all in range(own_blocks * QMAX))
     )
-    piece = lax.all_gather(white, "chan", axis=2, tiled=True)
+    size_2, place, span = (lax.axis_size("chan"), lax.axis_index("chan"), white.shape[2])
+    ahead = [(i_2, (i_2 + 1) % size_2) for i_2 in range(size_2)]
+    downward = [(i_2, (i_2 - 1) % size_2) for i_2 in range(size_2)]
+    result = jnp.zeros((*white.shape[:2], size_2 * span, *white.shape[2 + 1 :]), white.dtype)
+    result = lax.dynamic_update_slice_in_dim(result, white, place * span, axis=2)
+    from_left = from_right = white
+    halfway = size_2 // 2
+    for hop in range(1, halfway + 1):
+        from_left = lax.ppermute(from_left, "chan", ahead)
+        result = lax.dynamic_update_slice_in_dim(
+            result, from_left, (place - hop) % size_2 * span, axis=2
+        )
+        if hop < size_2 - halfway:
+            from_right = lax.ppermute(from_right, "chan", downward)
+            result = lax.dynamic_update_slice_in_dim(
+                result, from_right, (place + hop) % size_2 * span, axis=2
+            )
+    piece = result
     width = piece.shape[2]
     updated = []
     for slot_idx in range(QMAX):

time: 123 us -> 119 us (0.967)
  blocking collectives: 18.8 us -> 5.75 us
  waiting for transfers between devices: 42.2 us -> 48.1 us
  starting transfers between devices: 14.9 us -> 18.8 us
    all_gather x1 -> x0, blocking collectives: 13 us -> none  [shards(): piece = lax.all_gather(white, 'chan', axis=2, tiled=True)]
    ppermute x0 -> x3, waiting for transfers between devices: none -> 7.84 us  [the longest x2 7.84 us: shards(): from_left = lax.ppermute(from_left, 'chan', ahead)]
    ppermute x0 -> x3, starting transfers between devices: none -> 3.88 us  [the longest x1 2.16 us: shards(): from_right = lax.ppermute(from_right, 'chan', downward)]
    reduce_scatter x1, waiting for transfers between devices: 23.1 us -> 21.2 us  [shards(): lax.psum_scatter(stacked_cc, ('tm', 'band'), scatter_dimension=3, tiled=T...]
  transfers between devices with their start and end apart: 7 -> 10, of which waited for: 7 -> 9; matrix products, arithmetic and copies ran while one was open for 1% -> 2% of each run, Pallas kernels for 0% -> 0%
where the time goes in v1:
time: 119 us
  waiting for transfers between devices  48.1 us (40%)
  between operations  18.9 us (16%)
  starting transfers between devices  18.8 us (16%)
  matrix products  11.2 us (9%)
  other arithmetic  7.65 us (6%)
  local copies, waits for them, and re-layouts  6.7 us (6%)
  blocking collectives  5.75 us (5%)
  loops' own time  1.51 us (1%)
    reduce_scatter x1, waiting for transfers between devices, shards(): lax.psum_scatter(stacked_cc, ('tm', 'band'), scatter_dimension=3, tiled=T...  21.2 us
    ppermute x2, waiting for transfers between devices, padded_2(): lax.ppermute(lax.slice_in_dim(block, 0, width, axis=dim), axis, backward)  8.49 us
    ppermute x2, waiting for transfers between devices, shards(): from_left = lax.ppermute(from_left, 'chan', ahead)  7.84 us
    ppermute x2, starting transfers between devices, padded_2(): lax.ppermute(lax.slice_in_dim(block, block.shape[dim] - width, None, axis...  7.47 us
    psum x1, blocking collectives, shards(): power = lax.psum(local_power, ('tm', 'band'))  5.75 us
    dot_general x2, matrix products, one_piece(): lax.dot_general(jnp.sin(angle), normed, dims, precision=lax.Precision.HIG...  5.16 us
    dot_general x2, matrix products, one_piece(): lax.dot_general(jnp.cos(angle), normed, dims, precision=lax.Precision.HIG...  5.14 us
    reduce_scatter x1, waiting for transfers between devices, shards(): lax.psum_scatter(stacked.reshape(device_bins * lax.axis_size('tm'), 2, ch...  4.9 us
  transfers between devices with their start and end apart: 10, of which 9 were waited for; matrix products, arithmetic and copies ran while one was open for 2% of the time, Pallas kernels for 0%

profile of v1, /device:TPU:0, one launch (start us, length us, event | category | flops | bytes accessed | tf_op | source)
XLA Modules:
  0.0 118.6 jit_solution(10593670190951121607)
XLA Ops:
  6.5 0.9 slice.63
  7.5 4.8 %collective-permute-start = (f32[128,1]{1,0:T(8,128)S(1)}, f32[128,1]{1,0:T(8,128)S(1)}, u32[]{:S(2)}, u32[]{:S(2)}) collective-permute-start(f32[128,1]{1,0:T(8,128)S(1)} %slice.63), channel_id=1, source_target_pairs={{0,2},{1,3},{4,6},{5,7},{8,10},{9,11},{12,14},{13,15},{16,18},{17,... | collective-permute-start | bytes 1544 | tf_op jit(solution)/shard_map/ppermute | solution.py:17
  12.3 0.7 divide_exponential_fusion
  13.0 1.2 %collective-permute-done = f32[128,1]{1,0:T(8,128)S(1)} collective-permute-done((f32[128,1]{1,0:T(8,128)S(1)}, f32[128,1]{1,0:T(8,128)S(1)}, u32[]{:S(2)}, u32[]{:S(2)}) %collective-permute-start) | collective-permute-done | bytes 544 | tf_op jit(solution)/shard_map/ppermute | solution.py:17
  14.2 1.4 %fusion.34 = f32[128,1024]{1,0:T(8,128)S(1)} fusion(f32[128,1024]{1,0:T(8,128)} %param.13, f32[128,1023]{1,0:T(8,128)} %bitcast.94, f32[128,1]{1,0:T(8,128)S(1)} %collective-permute-done, f32[128]{0:T(128)S(1)} %divide_exponential_fusion), kind=kLoop, calls=%fused_computation.55 | loop fusion | flops 393216 | bytes 1573376 | tf_op jit(solution)/shard_map/sub | solution.py:74
  15.7 3.5 %collective-permute-start.1 = (f32[64,1024]{1,0:T(8,128)S(1)}, f32[64,1024]{1,0:T(8,128)S(1)}, u32[]{:S(2)}, u32[]{:S(2)}) collective-permute-start(f32[64,1024]{1,0:T(8,128)S(1)} %get-tuple-element.238), channel_id=1, source_target_pairs={{0,4},{4,8},{8,12},{1,5},{5,9},{9,13},{2,6},{6,10},{10,14},{3,7},{... | collective-permute-start | bytes 786440 | tf_op jit(solution)/shard_map/ppermute | solution.py:25
  19.2 1.3 %collective-permute-start.2 = (f32[64,1024]{1,0:T(8,128)S(1)}, f32[64,1024]{1,0:T(8,128)S(1)}, u32[]{:S(2)}, u32[]{:S(2)}) collective-permute-start(f32[64,1024]{1,0:T(8,128)S(1)} %get-tuple-element.239), channel_id=1, source_target_pairs={{4,0},{8,4},{12,8},{5,1},{9,5},{13,9},{6,2},{10,6},{14,10},{7,3},{... | collective-permute-start | bytes 786440 | tf_op jit(solution)/shard_map/ppermute | solution.py:28
  20.5 3.4 %collective-permute-done.1 = f32[64,1024]{1,0:T(8,128)S(1)} collective-permute-done((f32[64,1024]{1,0:T(8,128)S(1)}, f32[64,1024]{1,0:T(8,128)S(1)}, u32[]{:S(2)}, u32[]{:S(2)}) %collective-permute-start.1) | collective-permute-done | bytes 262176 | tf_op jit(solution)/shard_map/ppermute | solution.py:25
  23.9 4.1 %collective-permute-done.2 = f32[64,1024]{1,0:T(8,128)S(1)} collective-permute-done((f32[64,1024]{1,0:T(8,128)S(1)}, f32[64,1024]{1,0:T(8,128)S(1)}, u32[]{:S(2)}, u32[]{:S(2)}) %collective-permute-start.2) | collective-permute-done | bytes 262176 | tf_op jit(solution)/shard_map/ppermute | solution.py:28
  28.1 0.8 fusion.25
  29.6 4.0 %collective-permute-start.3 = (f32[128,256]{1,0:T(8,128)S(1)}, f32[128,256]{1,0:T(8,128)S(1)}, u32[]{:S(2)}, u32[]{:S(2)}) collective-permute-start(f32[128,256]{1,0:T(8,128)S(1)} %get-tuple-element.236), channel_id=1, source_target_pairs={{0,2},{1,3},{4,6},{5,7},{8,10},{9,11},{12,14},{13,15},{16,18},{17,... | collective-permute-start | bytes 393224 | tf_op jit(solution)/shard_map/ppermute | solution.py:25
  33.6 1.3 %collective-permute-start.4 = (f32[128,256]{1,0:T(8,128)S(1)}, f32[128,256]{1,0:T(8,128)S(1)}, u32[]{:S(2)}, u32[]{:S(2)}) collective-permute-start(f32[128,256]{1,0:T(8,128)S(1)} %get-tuple-element.237), channel_id=1, source_target_pairs={{2,0},{3,1},{6,4},{7,5},{10,8},{11,9},{14,12},{15,13},{18,16},{19,... | collective-permute-start | bytes 393224 | tf_op jit(solution)/shard_map/ppermute | solution.py:28
  34.9 1.1 collective-permute-done.3
  36.0 4.4 %collective-permute-done.4 = f32[128,256]{1,0:T(8,128)S(1)} collective-permute-done((f32[128,256]{1,0:T(8,128)S(1)}, f32[128,256]{1,0:T(8,128)S(1)}, u32[]{:S(2)}, u32[]{:S(2)}) %collective-permute-start.4) | collective-permute-done | bytes 131104 | tf_op jit(solution)/shard_map/ppermute | solution.py:28
  42.1 13.0 %while.13 = (s32[]{:T(128)}, f32[2,128,2,128]{3,1,0,2:T(8,128)S(1)}, s32[2]{0:T(128)S(1)}, s32[]{:T(128)}, f32[128,1024]{1,0:T(8,128)S(1)}, /*index=5*/s32[]{:T(128)}, s32[]{:T(128)}, s32[1]{0:T(128)}) while((s32[]{:T(128)}, f32[2,128,2,128]{3,1,0,2:T(8,128)S(1)}, s32[2]{0:T(128)S(1)}, s32[]{:T(128)}, f32[128,1024]{1,0:T(8,128)S(1)}, ...), condition=%wide.region_5.6_spmd.clone, body=%wide.region_4.5_spmd.clone.sunk | while | flops 406373504 | bytes 1455749 | solution.py:104
  42.1 0.6 dynamic_slice.42
  43.4 2.6 %convolution_bitcast_fusion.2 = f32[128,1,128]{2,0,1:T(8,128)S(1)} fusion(f32[128,1024]{1,0:T(8,128)S(1)} %get-tuple-element.307, s32[1024]{0:T(1024)S(1)} %iota_add_fusion.6, s32[128]{0:T(128)S(1)} %iota_add_fusion.7), kind=kOutput, calls=%fused_computation.15.clone.1 | convolution fusion | flops 203161600 | bytes 594432 | tf_op jit(solution)/shard_map/while/body/eval_jaxpr/dot_general | solution.py:88
  46.0 2.6 %fusion.64 = f32[128,1,128]{2,0,1:T(8,128)S(1)} fusion(f32[128,1024]{1,0:T(8,128)S(1)} %get-tuple-element.307, s32[1024]{0:T(1024)S(1)} %iota_add_fusion.6, s32[128]{0:T(128)S(1)} %iota_add_fusion.7), kind=kOutput, calls=%fused_computation.14.clone.1 | convolution fusion | flops 203177984 | bytes 594432 | tf_op jit(solution)/shard_map/while/body/eval_jaxpr/dot_general | solution.py:95
  49.9 2.6 %convolution_bitcast_fusion.2 = f32[128,1,128]{2,0,1:T(8,128)S(1)} fusion(f32[128,1024]{1,0:T(8,128)S(1)} %get-tuple-element.307, s32[1024]{0:T(1024)S(1)} %iota_add_fusion.6, s32[128]{0:T(128)S(1)} %iota_add_fusion.7), kind=kOutput, calls=%fused_computation.15.clone.1 | convolution fusion | flops 203161600 | bytes 594432 | tf_op jit(solution)/shard_map/while/body/eval_jaxpr/dot_general | solution.py:88
  52.5 2.6 %fusion.64 = f32[128,1,128]{2,0,1:T(8,128)S(1)} fusion(f32[128,1024]{1,0:T(8,128)S(1)} %get-tuple-element.307, s32[1024]{0:T(1024)S(1)} %iota_add_fusion.6, s32[128]{0:T(128)S(1)} %iota_add_fusion.7), kind=kOutput, calls=%fused_computation.14.clone.1 | convolution fusion | flops 203177984 | bytes 594432 | tf_op jit(solution)/shard_map/while/body/eval_jaxpr/dot_general | solution.py:95
  55.1 0.7 copy-done.1
  55.9 0.7 fusion.43
  62.0 4.9 %reduce-scatter.3.cloned.1.call-done = f32[128,2,128]{2,0,1:T(8,128)} async-done(((f32[256,2,128]{2,0,1:T(8,128)}), f32[128,2,128]{2,0,1:T(8,128)}) %reduce-scatter.3.cloned.1.call-update) | async-done | bytes 131088 | tf_op jit(solution)/shard_map/reduce_scatter | solution.py:105
  66.9 1.0 multiply_reduce_fusion
  67.9 5.8 %psum.7 = f32[128]{0:T(128)S(1)} all-reduce(f32[128]{0:T(128)S(1)} %multiply_reduce_fusion), channel_id=1, replica_groups=mesh['groups'=2,'chan'=4,'tm'=2,'band'=2] {'tm','band'}, use_global_device_ids=true, to_apply=%region_8.9 | all-reduce | flops 128 | bytes 1024 | tf_op jit(solution)/shard_map/psum | solution.py:112
  73.7 0.9 fusion.40
  74.6 1.7 %collective-permute-start.5 = (bf16[128,2,128]{2,0,1:T(8,128)(2,1)S(1)}, bf16[128,2,128]{2,0,1:T(8,128)(2,1)S(1)}, u32[]{:S(2)}, u32[]{:S(2)}) collective-permute-start(bf16[128,2,128]{2,0,1:T(8,128)(2,1)S(1)} %get-tuple-element.235), channel_id=1, source_target_pairs={{0,4},{4,8},{8,12},{12,0},{1,5},{5,9},{9,13},{13,1},{2,6},{6,10},{... | collective-permute-start | bytes 196616 | tf_op jit(solution)/shard_map/ppermute | solution.py:145
  76.3 2.2 %collective-permute-start.6 = (bf16[128,2,128]{2,0,1:T(8,128)(2,1)S(1)}, bf16[128,2,128]{2,0,1:T(8,128)(2,1)S(1)}, u32[]{:S(2)}, u32[]{:S(2)}) collective-permute-start(bf16[128,2,128]{2,0,1:T(8,128)(2,1)S(1)} %get-tuple-element.235), channel_id=1, source_target_pairs={{0,12},{4,0},{8,4},{12,8},{1,13},{5,1},{9,5},{13,9},{2,14},{6,2},{... | collective-permute-start | bytes 196616 | tf_op jit(solution)/shard_map/ppermute | solution.py:150
  79.3 2.0 %collective-permute-done.5 = bf16[128,2,128]{2,0,1:T(8,128)(2,1)S(1)} collective-permute-done((bf16[128,2,128]{2,0,1:T(8,128)(2,1)S(1)}, bf16[128,2,128]{2,0,1:T(8,128)(2,1)S(1)}, u32[]{:S(2)}, u32[]{:S(2)}) %collective-permute-start.5) | collective-permute-done | bytes 65568 | tf_op jit(solution)/shard_map/ppermute | solution.py:145
  81.6 5.8 %collective-permute-done.7 = bf16[128,2,128]{2,0,1:T(8,128)(2,1)S(1)} collective-permute-done((bf16[128,2,128]{2,0,1:T(8,128)(2,1)S(1)}, bf16[128,2,128]{2,0,1:T(8,128)(2,1)S(1)}, u32[]{:S(2)}, u32[]{:S(2)}) %collective-permute-start.7) | collective-permute-done | bytes 65568 | tf_op jit(solution)/shard_map/ppermute | solution.py:145
  89.6 0.9 pad_maximum_fusion.1
  90.6 21.2 %reduce-scatter.5.cloned.1.call-done = f32[1,4,3,32,128]{4,3,2,1,0:T(8,128)} async-done(((f32[1,4,3,128,128]{4,3,2,1,0:T(8,128)}), f32[1,4,3,32,128]{4,3,2,1,0:T(8,128)}) %reduce-scatter.5.cloned.1.call-update) | async-done | bytes 196624 | tf_op jit(solution)/shard_map/reduce_scatter | solution.py:178
  (70 shorter events, 8.7 us)
Async XLA Ops:
  6.5 28.4 %copy-start = (s32[4,4]{1,0:T(4,128)S(1)}, s32[4,4]{1,0:T(4,128)}, u32[]{:S(2)}) copy-start(s32[4,4]{1,0:T(4,128)} %param.15) | copy-start | bytes 196
  6.5 60.4 %reduce-scatter.3.cloned.1.call-start = ((), (), s32[]{:S(2)}) async-start(), calls=%async_computation.2 | async-start | bytes 393216 | tf_op jit(solution)/shard_map/reduce_scatter | solution.py:105
  7.5 6.7 %collective-permute-start = (f32[128,1]{1,0:T(8,128)S(1)}, f32[128,1]{1,0:T(8,128)S(1)}, u32[]{:S(2)}, u32[]{:S(2)}) collective-permute-start(f32[128,1]{1,0:T(8,128)S(1)} %slice.63), channel_id=1, source_target_pairs={{0,2},{1,3},{4,6},{5,7},{8,10},{9,11},{12,14},{13,15},{16,18},{17,... | collective-permute-start | bytes 1544 | tf_op jit(solution)/shard_map/ppermute | solution.py:17
  15.7 8.2 %collective-permute-start.1 = (f32[64,1024]{1,0:T(8,128)S(1)}, f32[64,1024]{1,0:T(8,128)S(1)}, u32[]{:S(2)}, u32[]{:S(2)}) collective-permute-start(f32[64,1024]{1,0:T(8,128)S(1)} %get-tuple-element.238), channel_id=1, source_target_pairs={{0,4},{4,8},{8,12},{1,5},{5,9},{9,13},{2,6},{6,10},{10,14},{3,7},{... | collective-permute-start | bytes 786440 | tf_op jit(solution)/shard_map/ppermute | solution.py:25
  19.2 8.8 %collective-permute-start.2 = (f32[64,1024]{1,0:T(8,128)S(1)}, f32[64,1024]{1,0:T(8,128)S(1)}, u32[]{:S(2)}, u32[]{:S(2)}) collective-permute-start(f32[64,1024]{1,0:T(8,128)S(1)} %get-tuple-element.239), channel_id=1, source_target_pairs={{4,0},{8,4},{12,8},{5,1},{9,5},{13,9},{6,2},{10,6},{14,10},{7,3},{... | collective-permute-start | bytes 786440 | tf_op jit(solution)/shard_map/ppermute | solution.py:28
  29.6 6.5 %collective-permute-start.3 = (f32[128,256]{1,0:T(8,128)S(1)}, f32[128,256]{1,0:T(8,128)S(1)}, u32[]{:S(2)}, u32[]{:S(2)}) collective-permute-start(f32[128,256]{1,0:T(8,128)S(1)} %get-tuple-element.236), channel_id=1, source_target_pairs={{0,2},{1,3},{4,6},{5,7},{8,10},{9,11},{12,14},{13,15},{16,18},{17,... | collective-permute-start | bytes 393224 | tf_op jit(solution)/shard_map/ppermute | solution.py:25
  33.6 6.9 %collective-permute-start.4 = (f32[128,256]{1,0:T(8,128)S(1)}, f32[128,256]{1,0:T(8,128)S(1)}, u32[]{:S(2)}, u32[]{:S(2)}) collective-permute-start(f32[128,256]{1,0:T(8,128)S(1)} %get-tuple-element.237), channel_id=1, source_target_pairs={{2,0},{3,1},{6,4},{7,5},{10,8},{11,9},{14,12},{15,13},{18,16},{19,... | collective-permute-start | bytes 393224 | tf_op jit(solution)/shard_map/ppermute | solution.py:28
  55.1 0.7 copy-start.1
  55.8 55.9 %reduce-scatter.5.cloned.1.call-start = ((), (), s32[]{:S(2)}) async-start(), calls=%async_computation.3 | async-start | bytes 983040 | tf_op jit(solution)/shard_map/reduce_scatter | solution.py:178
  74.6 6.8 %collective-permute-start.5 = (bf16[128,2,128]{2,0,1:T(8,128)(2,1)S(1)}, bf16[128,2,128]{2,0,1:T(8,128)(2,1)S(1)}, u32[]{:S(2)}, u32[]{:S(2)}) collective-permute-start(bf16[128,2,128]{2,0,1:T(8,128)(2,1)S(1)} %get-tuple-element.235), channel_id=1, source_target_pairs={{0,4},{4,8},{8,12},{12,0},{1,5},{5,9},{9,13},{13,1},{2,6},{6,10},{... | collective-permute-start | bytes 196616 | tf_op jit(solution)/shard_map/ppermute | solution.py:145
  76.3 5.2 %collective-permute-start.6 = (bf16[128,2,128]{2,0,1:T(8,128)(2,1)S(1)}, bf16[128,2,128]{2,0,1:T(8,128)(2,1)S(1)}, u32[]{:S(2)}, u32[]{:S(2)}) collective-permute-start(bf16[128,2,128]{2,0,1:T(8,128)(2,1)S(1)} %get-tuple-element.235), channel_id=1, source_target_pairs={{0,12},{4,0},{8,4},{12,8},{1,13},{5,1},{9,5},{13,9},{2,14},{6,2},{... | collective-permute-start | bytes 196616 | tf_op jit(solution)/shard_map/ppermute | solution.py:150
  81.4 6.1 %collective-permute-start.7 = (bf16[128,2,128]{2,0,1:T(8,128)(2,1)S(1)}, bf16[128,2,128]{2,0,1:T(8,128)(2,1)S(1)}, u32[]{:S(2)}, u32[]{:S(2)}) collective-permute-start(bf16[128,2,128]{2,0,1:T(8,128)(2,1)S(1)} %collective-permute-done.5), channel_id=1, source_target_pairs={{0,4},{4,8},{8,12},{12,0},{1,5},{5,9},{9,13},{13,1},{2,6},{6,10},{... | collective-permute-start | bytes 196616 | tf_op jit(solution)/shard_map/ppermute | solution.py:145
Sparse Core Ops, SparseCore 0:
  56.0 10.9 reduce-scatter.2
  90.7 20.9 reduce-scatter.4
